TPU v7x, 512 devices: a whole 4x4x16 slice. The times are simulated.
512 devices in a mesh: frame: 64 (over z, x), head: 8 (over y, core).
Axes of the slice: x: 4, y: 4, z: 16, core: 2. Of those that a mesh axis runs over, the one named last changes fastest.
Arguments:
- queries: bfloat16 [24576, 3072], P(('frame', 'head')), as said below
- key_vectors: bfloat16 [24576, 3072], P(('frame', 'head')), as said below
- value_vectors: bfloat16 [24576, 3072], P(('frame', 'head')), may hold values from -6 to 6
- windows: int32 [64, 27], P('frame'), may hold values from 0 to 63, as said below
- counts: int32 [64], P('frame'), may hold values from 1 to 27, as said below
Outputs:
- attended: bfloat16 [24576, 3072], P(('frame', 'head'))
Inputs may be any that keep to these rules, and one draw needn't show every extreme that they name: `windows`: tiles are numbered by layer, then row, then column in a grid of 4 x 4 x 4 tiles. Row t names tiles whose layer, row and column each differ from those of tile t by at most one; its first counts[t] entries are distinct and include t; the other entries equal t. `counts`: the number of live entries of each row of windows; some tile reaches 27 in every draw. `queries`: float entries; may be large in some rows. `key_vectors`: float entries.
All inputs are finite; a program needn't handle non-finite values.
Results may differ from a plain program's by a relative error of at most 0.012.
Values may be sent and summed in bfloat16 or wider, within the bound.
A program may use at most 128 MiB of HBM per device.

v0:
```python
import jax
import jax.numpy as jnp
from jax import lax
from jax.sharding import PartitionSpec as P

HEAD_DIM = 128
HT = 4
WT = 4


def passed_along(shard, axis, by):
    count = lax.axis_size(axis)
    pairs = [(i, i + by) for i in range(count) if 0 <= i + by < count]
    return lax.ppermute(shard, axis, pairs)


def neighbour_stack(paired):
    layer_step = HT * WT
    pieces = []
    for layer_move in (-1, 0, 1):
        for row_move in (-1, 0, 1):
            for column_move in (-1, 0, 1):
                offset = layer_move * layer_step + row_move * WT + column_move
                if offset == 0:
                    pieces.append(paired)
                else:
                    pieces.append(passed_along(paired, "frame", -offset))
    return jnp.stack(pieces)


def per_device(queries, key_vectors, value_vectors, windows, counts):
    exchanged = lax.all_to_all(
        jnp.stack([queries, key_vectors, value_vectors]),
        "head",
        split_axis=2,
        concat_axis=1,
        tiled=True,
    )
    local_query = exchanged[0]
    cube = neighbour_stack(exchanged[1:])
    tile_len = local_query.shape[0]
    width_local = local_query.shape[1]
    head_local = width_local // HEAD_DIM
    window_len = windows.shape[1]
    layer_size = HT * WT
    own_tile = lax.axis_index("frame")
    listed = windows[0]
    layer_diff = listed // layer_size - own_tile // layer_size
    row_diff = listed % layer_size // WT - own_tile % layer_size // WT
    column_diff = listed % WT - own_tile % WT
    slots = (layer_diff + 1) * 9 + (row_diff + 1) * 3 + (column_diff + 1)
    picked = cube[slots]
    key_flat = picked[:, 0].reshape(window_len * tile_len, width_local)
    value_flat = picked[:, 1].reshape(window_len * tile_len, width_local)
    usable = jnp.repeat(jnp.arange(window_len, dtype=jnp.int32) < counts[0], tile_len)
    inv_root = HEAD_DIM ** (-0.5)
    block_rows = tile_len // 4

    def one_head(head_number):
        start = head_number * HEAD_DIM
        key_one = lax.dynamic_slice_in_dim(key_flat, start, HEAD_DIM, 1)
        value_one = lax.dynamic_slice_in_dim(value_flat, start, HEAD_DIM, 1)
        query_one = lax.dynamic_slice_in_dim(local_query, start, HEAD_DIM, 1)
        query_blocks = query_one.reshape(4, block_rows, HEAD_DIM)

        def attend(query_block):
            scores = (
                lax.dot_general(
                    query_block,
                    key_one,
                    (((1,), (1,)), ((), ())),
                    preferred_element_type=jnp.float32,
                )
                * inv_root
            )
            scores = jnp.where(usable[None, :], scores, jnp.float32(-1e30))
            row_max = jnp.max(scores, axis=1, keepdims=True)
            raised = jnp.exp(scores - row_max)
            weights = (raised / jnp.sum(raised, axis=1, keepdims=True)).astype(jnp.bfloat16)
            return jnp.dot(weights, value_one, preferred_element_type=jnp.float32).astype(
                jnp.bfloat16
            )

        return lax.map(attend, query_blocks).reshape(tile_len, HEAD_DIM)

    result = lax.map(one_head, jnp.arange(head_local, dtype=jnp.int32))
    attended = result.transpose(1, 0, 2).reshape(tile_len, width_local)
    return lax.all_to_all(attended, "head", split_axis=0, concat_axis=1, tiled=True)


def solution(mesh):
    placed = (
        P(("frame", "head"), None),
        P(("frame", "head"), None),
        P(("frame", "head"), None),
        P("frame", None),
        P("frame"),
    )
    return jax.shard_map(
        per_device,
        mesh=mesh,
        in_specs=placed,
        out_specs=P(("frame", "head"), None),
        check_vma=False,
    )
```

profile of v0, /device:TPU:103, one launch (start us, length us, event | category | flops | bytes accessed | tf_op | source)
XLA Modules:
  0.0 1292.8 jit_solution(9733887223938937551)
XLA Ops:
  2.2 4.5 copy.18
  6.7 4.8 reshape.240
  11.5 18.7 %all_to_all.34 = bf16[8,2,27648]{2,1,0:T(2,128)(2,1)} all-to-all(bf16[8,2,27648]{2,1,0:T(2,128)(2,1)} %reshape.240), channel_id=1, replica_groups=mesh['frame'=64,'head'=8] {'head'}, dimensions={0} | all-to-all | bytes 1769472 | tf_op jit(solution)/shard_map/all_to_all | solution.py:32
  30.3 6.1 reshape.241
  36.4 3.1 copy.19
  40.6 11.8 collective-permute-start
  52.5 4.5 collective-permute-start.1
  64.3 254.0 %collective-permute-done = bf16[2,384,384]{2,1,0:T(8,128)(2,1)S(1)} collective-permute-done((bf16[2,384,384]{2,1,0:T(8,128)(2,1)S(1)}, bf16[2,384,384]{2,1,0:T(8,128)(2,1)S(1)}, u32[]{:S(2)}, u32[]{:S(2)}) %collective-permute-start) | collective-permute-done | bytes 589856 | tf_op jit(solution)/shard_map/ppermute | solution.py:14
  321.1 35.6 %collective-permute-done.1 = bf16[2,384,384]{2,1,0:T(8,128)(2,1)S(1)} collective-permute-done((bf16[2,384,384]{2,1,0:T(8,128)(2,1)S(1)}, bf16[2,384,384]{2,1,0:T(8,128)(2,1)S(1)}, u32[]{:S(2)}, u32[]{:S(2)}) %collective-permute-start.1) | collective-permute-done | bytes 589856 | tf_op jit(solution)/shard_map/ppermute | solution.py:14
  359.5 9.8 collective-permute-done.2
  372.1 9.8 collective-permute-done.3
  382.0 54.2 %collective-permute-start.8 = (bf16[2,384,384]{2,1,0:T(8,128)(2,1)S(1)}, bf16[2,384,384]{2,1,0:T(8,128)(2,1)S(1)}, u32[]{:S(2)}, u32[]{:S(2)}) collective-permute-start(bf16[2,384,384]{2,1,0:T(8,128)(2,1)S(1)} %bitcast.140), channel_id=1, source_target_pairs={{0,88},{8,96},{16,104},{24,112},{32,120},{40,128},{48,136},{56,144... | collective-permute-start | bytes 1769480 | tf_op jit(solution)/shard_map/ppermute | solution.py:14
  439.8 14.1 %collective-permute-done.5 = bf16[2,384,384]{2,1,0:T(8,128)(2,1)S(1)} collective-permute-done((bf16[2,384,384]{2,1,0:T(8,128)(2,1)S(1)}, bf16[2,384,384]{2,1,0:T(8,128)(2,1)S(1)}, u32[]{:S(2)}, u32[]{:S(2)}) %collective-permute-start.5) | collective-permute-done | bytes 589856 | tf_op jit(solution)/shard_map/ppermute | solution.py:14
  454.0 67.3 %collective-permute-start.10 = (bf16[2,384,384]{2,1,0:T(8,128)(2,1)S(1)}, bf16[2,384,384]{2,1,0:T(8,128)(2,1)S(1)}, u32[]{:S(2)}, u32[]{:S(2)}) collective-permute-start(bf16[2,384,384]{2,1,0:T(8,128)(2,1)S(1)} %bitcast.142), channel_id=1, source_target_pairs={{0,32},{8,40},{16,48},{24,56},{32,64},{40,72},{48,80},{56,88},{64,... | collective-permute-start | bytes 1769480 | tf_op jit(solution)/shard_map/ppermute | solution.py:14
  525.0 14.1 %collective-permute-start.12 = (bf16[2,384,384]{2,1,0:T(8,128)(2,1)S(1)}, bf16[2,384,384]{2,1,0:T(8,128)(2,1)S(1)}, u32[]{:S(2)}, u32[]{:S(2)}) collective-permute-start(bf16[2,384,384]{2,1,0:T(8,128)(2,1)S(1)} %bitcast.144), channel_id=1, source_target_pairs={{0,8},{8,16},{16,24},{24,32},{32,40},{40,48},{48,56},{56,64},{64,7... | collective-permute-start | bytes 1769480 | tf_op jit(solution)/shard_map/ppermute | solution.py:14
  551.2 7.4 collective-permute-done.12
  569.0 28.6 %collective-permute-done.15 = bf16[2,384,384]{2,1,0:T(8,128)(2,1)S(1)} collective-permute-done((bf16[2,384,384]{2,1,0:T(8,128)(2,1)S(1)}, bf16[2,384,384]{2,1,0:T(8,128)(2,1)S(1)}, u32[]{:S(2)}, u32[]{:S(2)}) %collective-permute-start.15) | collective-permute-done | bytes 589856 | tf_op jit(solution)/shard_map/ppermute | solution.py:14
  600.5 12.8 collective-permute-done.16
  615.4 48.3 %collective-permute-done.17 = bf16[2,384,384]{2,1,0:T(8,128)(2,1)S(1)} collective-permute-done((bf16[2,384,384]{2,1,0:T(8,128)(2,1)S(1)}, bf16[2,384,384]{2,1,0:T(8,128)(2,1)S(1)}, u32[]{:S(2)}, u32[]{:S(2)}) %collective-permute-start.17) | collective-permute-done | bytes 589856 | tf_op jit(solution)/shard_map/ppermute | solution.py:14
  665.9 22.0 %collective-permute-done.18 = bf16[2,384,384]{2,1,0:T(8,128)(2,1)S(1)} collective-permute-done((bf16[2,384,384]{2,1,0:T(8,128)(2,1)S(1)}, bf16[2,384,384]{2,1,0:T(8,128)(2,1)S(1)}, u32[]{:S(2)}, u32[]{:S(2)}) %collective-permute-start.18) | collective-permute-done | bytes 589856 | tf_op jit(solution)/shard_map/ppermute | solution.py:14
  690.1 30.8 %collective-permute-done.19 = bf16[2,384,384]{2,1,0:T(8,128)(2,1)S(1)} collective-permute-done((bf16[2,384,384]{2,1,0:T(8,128)(2,1)S(1)}, bf16[2,384,384]{2,1,0:T(8,128)(2,1)S(1)}, u32[]{:S(2)}, u32[]{:S(2)}) %collective-permute-start.19) | collective-permute-done | bytes 589856 | tf_op jit(solution)/shard_map/ppermute | solution.py:14
  723.0 25.0 %collective-permute-done.20 = bf16[2,384,384]{2,1,0:T(8,128)(2,1)S(1)} collective-permute-done((bf16[2,384,384]{2,1,0:T(8,128)(2,1)S(1)}, bf16[2,384,384]{2,1,0:T(8,128)(2,1)S(1)}, u32[]{:S(2)}, u32[]{:S(2)}) %collective-permute-start.20) | collective-permute-done | bytes 589856 | tf_op jit(solution)/shard_map/ppermute | solution.py:14
  750.3 30.8 %collective-permute-done.21 = bf16[2,384,384]{2,1,0:T(8,128)(2,1)S(1)} collective-permute-done((bf16[2,384,384]{2,1,0:T(8,128)(2,1)S(1)}, bf16[2,384,384]{2,1,0:T(8,128)(2,1)S(1)}, u32[]{:S(2)}, u32[]{:S(2)}) %collective-permute-start.21) | collective-permute-done | bytes 589856 | tf_op jit(solution)/shard_map/ppermute | solution.py:14
  782.0 141.4 %collective-permute-done.22 = bf16[2,384,384]{2,1,0:T(8,128)(2,1)S(1)} collective-permute-done((bf16[2,384,384]{2,1,0:T(8,128)(2,1)S(1)}, bf16[2,384,384]{2,1,0:T(8,128)(2,1)S(1)}, u32[]{:S(2)}, u32[]{:S(2)}) %collective-permute-start.22) | collective-permute-done | bytes 589856 | tf_op jit(solution)/shard_map/ppermute | solution.py:14
  924.3 48.2 %collective-permute-done.23 = bf16[2,384,384]{2,1,0:T(8,128)(2,1)S(1)} collective-permute-done((bf16[2,384,384]{2,1,0:T(8,128)(2,1)S(1)}, bf16[2,384,384]{2,1,0:T(8,128)(2,1)S(1)}, u32[]{:S(2)}, u32[]{:S(2)}) %collective-permute-start.23) | collective-permute-done | bytes 589856 | tf_op jit(solution)/shard_map/ppermute | solution.py:14
  973.4 27.0 %collective-permute-done.24 = bf16[2,384,384]{2,1,0:T(8,128)(2,1)S(1)} collective-permute-done((bf16[2,384,384]{2,1,0:T(8,128)(2,1)S(1)}, bf16[2,384,384]{2,1,0:T(8,128)(2,1)S(1)}, u32[]{:S(2)}, u32[]{:S(2)}) %collective-permute-start.24) | collective-permute-done | bytes 589856 | tf_op jit(solution)/shard_map/ppermute | solution.py:14
  1001.2 182.6 %collective-permute-done.25 = bf16[2,384,384]{2,1,0:T(8,128)(2,1)S(1)} collective-permute-done((bf16[2,384,384]{2,1,0:T(8,128)(2,1)S(1)}, bf16[2,384,384]{2,1,0:T(8,128)(2,1)S(1)}, u32[]{:S(2)}, u32[]{:S(2)}) %collective-permute-start.25) | collective-permute-done | bytes 589856 | tf_op jit(solution)/shard_map/ppermute | solution.py:14
  1184.7 12.9 gather_fusion
  1197.6 11.4 fusion.13
  1208.9 72.4 %while.24 = (s32[]{:T(128)}, bf16[3,384,128]{2,1,0:T(8,128)(2,1)S(1)}, s32[3]{0:T(128)S(1)}, bf16[384,384]{1,0:T(8,128)(2,1)S(1)}, bf16[10368,384]{1,0:T(8,128)(...) while((s32[]{:T(128)}, ...), condition=%wide.region_5.6_spmd.clone, body=%wide.region_0.5_spmd.clone.sunk | while | flops 517582656 | bytes 28397988 | solution.py:86
  1210.4 3.8 constant_dynamic-slice_fusion.6
  1214.2 18.8 %while.25 = (s32[]{:T(128)}, bf16[4,96,128]{2,1,0:T(8,128)(2,1)S(1)}, pred[27,384]{1,0:T(8,128)(4,1)}, bf16[4,96,128]{2,1,0:T(8,128)(2,1)S(1)}, bf16[10368,128]{...) while((s32[]{:T(128)}, ...), condition=%wide.wide.region_4.4_spmd, body=%wide.wide.region_1.3_spmd.sunk | while | flops 517582656 | bytes 17315044 | solution.py:84
  1216.1 2.8 fusion.30
  1225.5 2.8 fusion.30
  1230.2 2.8 fusion.30
  1234.5 3.8 constant_dynamic-slice_fusion.6
  1238.3 18.8 %while.25 = (s32[]{:T(128)}, bf16[4,96,128]{2,1,0:T(8,128)(2,1)S(1)}, pred[27,384]{1,0:T(8,128)(4,1)}, bf16[4,96,128]{2,1,0:T(8,128)(2,1)S(1)}, bf16[10368,128]{...) while((s32[]{:T(128)}, ...), condition=%wide.wide.region_4.4_spmd, body=%wide.wide.region_1.3_spmd.sunk | while | flops 517582656 | bytes 17315044 | solution.py:84
  1240.2 2.8 fusion.30
  1245.0 2.8 fusion.30
  1249.7 2.8 fusion.30
  1254.4 2.8 fusion.30
  1258.7 3.8 constant_dynamic-slice_fusion.6
  1262.5 18.8 %while.25 = (s32[]{:T(128)}, bf16[4,96,128]{2,1,0:T(8,128)(2,1)S(1)}, pred[27,384]{1,0:T(8,128)(4,1)}, bf16[4,96,128]{2,1,0:T(8,128)(2,1)S(1)}, bf16[10368,128]{...) while((s32[]{:T(128)}, ...), condition=%wide.wide.region_4.4_spmd, body=%wide.wide.region_1.3_spmd.sunk | while | flops 517582656 | bytes 17315044 | solution.py:84
  1264.4 2.8 fusion.30
  1269.1 2.8 fusion.30
  1273.8 2.8 fusion.30
  1278.5 2.8 fusion.30
  1281.9 10.2 all_to_all.35
  (119 shorter events, 95.4 us)
Async XLA Ops:
  0.0 57.0 %copy-start.1 = (s32[1,27]{1,0:T(1,128)S(1)}, s32[1,27]{1,0:T(1,128)}, u32[]{:S(2)}) copy-start(s32[1,27]{1,0:T(1,128)} %param.12) | copy-start | bytes 328
  40.6 277.7 %collective-permute-start = (bf16[2,384,384]{2,1,0:T(8,128)(2,1)S(1)}, bf16[2,384,384]{2,1,0:T(8,128)(2,1)S(1)}, u32[]{:S(2)}, u32[]{:S(2)}) collective-permute-start(bf16[2,384,384]{2,1,0:T(8,128)(2,1)S(1)} %bitcast.132), channel_id=1, source_target_pairs={{0,168},{8,176},{16,184},{24,192},{32,200},{40,208},{48,216},{56,2... | collective-permute-start | bytes 1769480 | tf_op jit(solution)/shard_map/ppermute | solution.py:14
  52.5 304.2 %collective-permute-start.1 = (bf16[2,384,384]{2,1,0:T(8,128)(2,1)S(1)}, bf16[2,384,384]{2,1,0:T(8,128)(2,1)S(1)}, u32[]{:S(2)}, u32[]{:S(2)}) collective-permute-start(bf16[2,384,384]{2,1,0:T(8,128)(2,1)S(1)} %bitcast.133), channel_id=1, source_target_pairs={{0,160},{8,168},{16,176},{24,184},{32,192},{40,200},{48,208},{56,2... | collective-permute-start | bytes 1769480 | tf_op jit(solution)/shard_map/ppermute | solution.py:14
  57.7 311.7 %collective-permute-start.2 = (bf16[2,384,384]{2,1,0:T(8,128)(2,1)S(1)}, bf16[2,384,384]{2,1,0:T(8,128)(2,1)S(1)}, u32[]{:S(2)}, u32[]{:S(2)}) collective-permute-start(bf16[2,384,384]{2,1,0:T(8,128)(2,1)S(1)} %bitcast.134), channel_id=1, source_target_pairs={{0,152},{8,160},{16,168},{24,176},{32,184},{40,192},{48,200},{56,2... | collective-permute-start | bytes 1769480 | tf_op jit(solution)/shard_map/ppermute | solution.py:14
  61.1 320.9 %collective-permute-start.3 = (bf16[2,384,384]{2,1,0:T(8,128)(2,1)S(1)}, bf16[2,384,384]{2,1,0:T(8,128)(2,1)S(1)}, u32[]{:S(2)}, u32[]{:S(2)}) collective-permute-start(bf16[2,384,384]{2,1,0:T(8,128)(2,1)S(1)} %bitcast.135), channel_id=1, source_target_pairs={{0,136},{8,144},{16,152},{24,160},{32,168},{40,176},{48,184},{56,1... | collective-permute-start | bytes 1769480 | tf_op jit(solution)/shard_map/ppermute | solution.py:14
  63.0 374.0 %collective-permute-start.4 = (bf16[2,384,384]{2,1,0:T(8,128)(2,1)S(1)}, bf16[2,384,384]{2,1,0:T(8,128)(2,1)S(1)}, u32[]{:S(2)}, u32[]{:S(2)}) collective-permute-start(bf16[2,384,384]{2,1,0:T(8,128)(2,1)S(1)} %bitcast.136), channel_id=1, source_target_pairs={{0,128},{8,136},{16,144},{24,152},{32,160},{40,168},{48,176},{56,1... | collective-permute-start | bytes 1769480 | tf_op jit(solution)/shard_map/ppermute | solution.py:14
  318.3 135.6 %collective-permute-start.5 = (bf16[2,384,384]{2,1,0:T(8,128)(2,1)S(1)}, bf16[2,384,384]{2,1,0:T(8,128)(2,1)S(1)}, u32[]{:S(2)}, u32[]{:S(2)}) collective-permute-start(bf16[2,384,384]{2,1,0:T(8,128)(2,1)S(1)} %bitcast.137), channel_id=1, source_target_pairs={{0,120},{8,128},{16,136},{24,144},{32,152},{40,160},{48,168},{56,1... | collective-permute-start | bytes 1769480 | tf_op jit(solution)/shard_map/ppermute | solution.py:14
  356.7 165.5 %collective-permute-start.6 = (bf16[2,384,384]{2,1,0:T(8,128)(2,1)S(1)}, bf16[2,384,384]{2,1,0:T(8,128)(2,1)S(1)}, u32[]{:S(2)}, u32[]{:S(2)}) collective-permute-start(bf16[2,384,384]{2,1,0:T(8,128)(2,1)S(1)} %bitcast.138), channel_id=1, source_target_pairs={{0,104},{8,112},{16,120},{24,128},{32,136},{40,144},{48,152},{56,1... | collective-permute-start | bytes 1769480 | tf_op jit(solution)/shard_map/ppermute | solution.py:14
  369.3 155.6 %collective-permute-start.7 = (bf16[2,384,384]{2,1,0:T(8,128)(2,1)S(1)}, bf16[2,384,384]{2,1,0:T(8,128)(2,1)S(1)}, u32[]{:S(2)}, u32[]{:S(2)}) collective-permute-start(bf16[2,384,384]{2,1,0:T(8,128)(2,1)S(1)} %bitcast.139), channel_id=1, source_target_pairs={{0,96},{8,104},{16,112},{24,120},{32,128},{40,136},{48,144},{56,15... | collective-permute-start | bytes 1769480 | tf_op jit(solution)/shard_map/ppermute | solution.py:14
  382.0 158.0 %collective-permute-start.8 = (bf16[2,384,384]{2,1,0:T(8,128)(2,1)S(1)}, bf16[2,384,384]{2,1,0:T(8,128)(2,1)S(1)}, u32[]{:S(2)}, u32[]{:S(2)}) collective-permute-start(bf16[2,384,384]{2,1,0:T(8,128)(2,1)S(1)} %bitcast.140), channel_id=1, source_target_pairs={{0,88},{8,96},{16,104},{24,112},{32,120},{40,128},{48,136},{56,144... | collective-permute-start | bytes 1769480 | tf_op jit(solution)/shard_map/ppermute | solution.py:14
  437.0 105.7 %collective-permute-start.9 = (bf16[2,384,384]{2,1,0:T(8,128)(2,1)S(1)}, bf16[2,384,384]{2,1,0:T(8,128)(2,1)S(1)}, u32[]{:S(2)}, u32[]{:S(2)}) collective-permute-start(bf16[2,384,384]{2,1,0:T(8,128)(2,1)S(1)} %bitcast.141), channel_id=1, source_target_pairs={{0,40},{8,48},{16,56},{24,64},{32,72},{40,80},{48,88},{56,96},{64,... | collective-permute-start | bytes 1769480 | tf_op jit(solution)/shard_map/ppermute | solution.py:14
  454.0 91.6 %collective-permute-start.10 = (bf16[2,384,384]{2,1,0:T(8,128)(2,1)S(1)}, bf16[2,384,384]{2,1,0:T(8,128)(2,1)S(1)}, u32[]{:S(2)}, u32[]{:S(2)}) collective-permute-start(bf16[2,384,384]{2,1,0:T(8,128)(2,1)S(1)} %bitcast.142), channel_id=1, source_target_pairs={{0,32},{8,40},{16,48},{24,56},{32,64},{40,72},{48,80},{56,88},{64,... | collective-permute-start | bytes 1769480 | tf_op jit(solution)/shard_map/ppermute | solution.py:14
  522.2 26.2 %collective-permute-start.11 = (bf16[2,384,384]{2,1,0:T(8,128)(2,1)S(1)}, bf16[2,384,384]{2,1,0:T(8,128)(2,1)S(1)}, u32[]{:S(2)}, u32[]{:S(2)}) collective-permute-start(bf16[2,384,384]{2,1,0:T(8,128)(2,1)S(1)} %bitcast.143), channel_id=1, source_target_pairs={{0,24},{8,32},{16,40},{24,48},{32,56},{40,64},{48,72},{56,80},{64,... | collective-permute-start | bytes 1769480 | tf_op jit(solution)/shard_map/ppermute | solution.py:14
  525.0 33.7 %collective-permute-start.12 = (bf16[2,384,384]{2,1,0:T(8,128)(2,1)S(1)}, bf16[2,384,384]{2,1,0:T(8,128)(2,1)S(1)}, u32[]{:S(2)}, u32[]{:S(2)}) collective-permute-start(bf16[2,384,384]{2,1,0:T(8,128)(2,1)S(1)} %bitcast.144), channel_id=1, source_target_pairs={{0,8},{8,16},{16,24},{24,32},{32,40},{40,48},{48,56},{56,64},{64,7... | collective-permute-start | bytes 1769480 | tf_op jit(solution)/shard_map/ppermute | solution.py:14
  540.0 22.3 %collective-permute-start.13 = (bf16[2,384,384]{2,1,0:T(8,128)(2,1)S(1)}, bf16[2,384,384]{2,1,0:T(8,128)(2,1)S(1)}, u32[]{:S(2)}, u32[]{:S(2)}) collective-permute-start(bf16[2,384,384]{2,1,0:T(8,128)(2,1)S(1)} %bitcast.145), channel_id=1, source_target_pairs={{8,0},{16,8},{24,16},{32,24},{40,32},{48,40},{56,48},{64,56},{72,6... | collective-permute-start | bytes 1769480 | tf_op jit(solution)/shard_map/ppermute | solution.py:14
  542.8 23.4 %collective-permute-start.14 = (bf16[2,384,384]{2,1,0:T(8,128)(2,1)S(1)}, bf16[2,384,384]{2,1,0:T(8,128)(2,1)S(1)}, u32[]{:S(2)}, u32[]{:S(2)}) collective-permute-start(bf16[2,384,384]{2,1,0:T(8,128)(2,1)S(1)} %bitcast.146), channel_id=1, source_target_pairs={{24,0},{32,8},{40,16},{48,24},{56,32},{64,40},{72,48},{80,56},{88,... | collective-permute-start | bytes 1769480 | tf_op jit(solution)/shard_map/ppermute | solution.py:14
  545.6 52.0 %collective-permute-start.15 = (bf16[2,384,384]{2,1,0:T(8,128)(2,1)S(1)}, bf16[2,384,384]{2,1,0:T(8,128)(2,1)S(1)}, u32[]{:S(2)}, u32[]{:S(2)}) collective-permute-start(bf16[2,384,384]{2,1,0:T(8,128)(2,1)S(1)} %bitcast.147), channel_id=1, source_target_pairs={{32,0},{40,8},{48,16},{56,24},{64,32},{72,40},{80,48},{88,56},{96,... | collective-permute-start | bytes 1769480 | tf_op jit(solution)/shard_map/ppermute | solution.py:14
  548.4 64.9 %collective-permute-start.16 = (bf16[2,384,384]{2,1,0:T(8,128)(2,1)S(1)}, bf16[2,384,384]{2,1,0:T(8,128)(2,1)S(1)}, u32[]{:S(2)}, u32[]{:S(2)}) collective-permute-start(bf16[2,384,384]{2,1,0:T(8,128)(2,1)S(1)} %bitcast.148), channel_id=1, source_target_pairs={{40,0},{48,8},{56,16},{64,24},{72,32},{80,40},{88,48},{96,56},{104... | collective-permute-start | bytes 1769480 | tf_op jit(solution)/shard_map/ppermute | solution.py:14
  558.6 105.1 %collective-permute-start.17 = (bf16[2,384,384]{2,1,0:T(8,128)(2,1)S(1)}, bf16[2,384,384]{2,1,0:T(8,128)(2,1)S(1)}, u32[]{:S(2)}, u32[]{:S(2)}) collective-permute-start(bf16[2,384,384]{2,1,0:T(8,128)(2,1)S(1)} %bitcast.149), channel_id=1, source_target_pairs={{88,0},{96,8},{104,16},{112,24},{120,32},{128,40},{136,48},{144,56... | collective-permute-start | bytes 1769480 | tf_op jit(solution)/shard_map/ppermute | solution.py:14
  562.3 125.6 %collective-permute-start.18 = (bf16[2,384,384]{2,1,0:T(8,128)(2,1)S(1)}, bf16[2,384,384]{2,1,0:T(8,128)(2,1)S(1)}, u32[]{:S(2)}, u32[]{:S(2)}) collective-permute-start(bf16[2,384,384]{2,1,0:T(8,128)(2,1)S(1)} %bitcast.151), channel_id=1, source_target_pairs={{96,0},{104,8},{112,16},{120,24},{128,32},{136,40},{144,48},{152,5... | collective-permute-start | bytes 1769480 | tf_op jit(solution)/shard_map/ppermute | solution.py:14
  566.1 154.7 %collective-permute-start.19 = (bf16[2,384,384]{2,1,0:T(8,128)(2,1)S(1)}, bf16[2,384,384]{2,1,0:T(8,128)(2,1)S(1)}, u32[]{:S(2)}, u32[]{:S(2)}) collective-permute-start(bf16[2,384,384]{2,1,0:T(8,128)(2,1)S(1)} %bitcast.152), channel_id=1, source_target_pairs={{104,0},{112,8},{120,16},{128,24},{136,32},{144,40},{152,48},{160,... | collective-permute-start | bytes 1769480 | tf_op jit(solution)/shard_map/ppermute | solution.py:14
  597.6 150.3 %collective-permute-start.20 = (bf16[2,384,384]{2,1,0:T(8,128)(2,1)S(1)}, bf16[2,384,384]{2,1,0:T(8,128)(2,1)S(1)}, u32[]{:S(2)}, u32[]{:S(2)}) collective-permute-start(bf16[2,384,384]{2,1,0:T(8,128)(2,1)S(1)} %bitcast.153), channel_id=1, source_target_pairs={{120,0},{128,8},{136,16},{144,24},{152,32},{160,40},{168,48},{176,... | collective-permute-start | bytes 1769480 | tf_op jit(solution)/shard_map/ppermute | solution.py:14
  613.3 167.8 %collective-permute-start.21 = (bf16[2,384,384]{2,1,0:T(8,128)(2,1)S(1)}, bf16[2,384,384]{2,1,0:T(8,128)(2,1)S(1)}, u32[]{:S(2)}, u32[]{:S(2)}) collective-permute-start(bf16[2,384,384]{2,1,0:T(8,128)(2,1)S(1)} %bitcast.154), channel_id=1, source_target_pairs={{128,0},{136,8},{144,16},{152,24},{160,32},{168,40},{176,48},{184,... | collective-permute-start | bytes 1769480 | tf_op jit(solution)/shard_map/ppermute | solution.py:14
  663.8 259.6 %collective-permute-start.22 = (bf16[2,384,384]{2,1,0:T(8,128)(2,1)S(1)}, bf16[2,384,384]{2,1,0:T(8,128)(2,1)S(1)}, u32[]{:S(2)}, u32[]{:S(2)}) collective-permute-start(bf16[2,384,384]{2,1,0:T(8,128)(2,1)S(1)} %bitcast.155), channel_id=1, source_target_pairs={{136,0},{144,8},{152,16},{160,24},{168,32},{176,40},{184,48},{192,... | collective-permute-start | bytes 1769480 | tf_op jit(solution)/shard_map/ppermute | solution.py:14
  687.9 284.6 %collective-permute-start.23 = (bf16[2,384,384]{2,1,0:T(8,128)(2,1)S(1)}, bf16[2,384,384]{2,1,0:T(8,128)(2,1)S(1)}, u32[]{:S(2)}, u32[]{:S(2)}) collective-permute-start(bf16[2,384,384]{2,1,0:T(8,128)(2,1)S(1)} %bitcast.156), channel_id=1, source_target_pairs={{152,0},{160,8},{168,16},{176,24},{184,32},{192,40},{200,48},{208,... | collective-permute-start | bytes 1769480 | tf_op jit(solution)/shard_map/ppermute | solution.py:14
  720.8 279.5 %collective-permute-start.24 = (bf16[2,384,384]{2,1,0:T(8,128)(2,1)S(1)}, bf16[2,384,384]{2,1,0:T(8,128)(2,1)S(1)}, u32[]{:S(2)}, u32[]{:S(2)}) collective-permute-start(bf16[2,384,384]{2,1,0:T(8,128)(2,1)S(1)} %bitcast.157), channel_id=1, source_target_pairs={{160,0},{168,8},{176,16},{184,24},{192,32},{200,40},{208,48},{216,... | collective-permute-start | bytes 1769480 | tf_op jit(solution)/shard_map/ppermute | solution.py:14
  748.0 435.8 %collective-permute-start.25 = (bf16[2,384,384]{2,1,0:T(8,128)(2,1)S(1)}, bf16[2,384,384]{2,1,0:T(8,128)(2,1)S(1)}, u32[]{:S(2)}, u32[]{:S(2)}) collective-permute-start(bf16[2,384,384]{2,1,0:T(8,128)(2,1)S(1)} %bitcast.158), channel_id=1, source_target_pairs={{168,0},{176,8},{184,16},{192,24},{200,32},{208,40},{216,48},{224,... | collective-permute-start | bytes 1769480 | tf_op jit(solution)/shard_map/ppermute | solution.py:14
  1209.0 5.2 copy-start
  1233.2 5.2 copy-start
  1257.3 5.2 copy-start
where the time goes:
time: 1290 us
  waiting for transfers between devices  929 us (72%)
  starting transfers between devices  189 us (15%)
  local copies, waits for them, and re-layouts  84 us (7%)
  matrix products  46.6 us (4%)
  blocking collectives  28.9 us (2%)
    ppermute x26, waiting for transfers between devices, passed_along(): return lax.ppermute(shard, axis, pairs)  929 us
    ppermute x26, starting transfers between devices, passed_along(): return lax.ppermute(shard, axis, pairs)  189 us
    unnamed x30, local copies, waits for them, and re-layouts  34.1 us
    dot_general x12, matrix products, attend(): jnp.dot(weights, value_one, preferred_element_type=jnp.float32)  33.6 us
  transfers between devices with their start and end apart: 26, of which 18 were waited for; matrix products, arithmetic and copies ran while one was open for 2% of the time, Pallas kernels for 0%

commit v1 on v0

v1 whole, which is shorter than its diff:
```python
import functools

import jax
import jax.numpy as jnp
from jax import lax
from jax.experimental import pallas as pl
from jax.experimental.pallas import tpu as pltpu
from jax.sharding import PartitionSpec as P

HEAD_DIM = 128
HT = 4
WT = 4
CORES = 2
FLAG_ROWS = 32
SUM_ROWS = 16
LOW = -3.0e38
EXPONENT_SCALE = HEAD_DIM ** (-0.5) * 1.4426950408889634
MESH = pl.DeviceIdType.MESH


def kernel(
    rows_of_tiles,
    frames,
    parts,
    windows,
    counts,
    queries,
    keys,
    values,
    out,
    kv,
    value_stage,
    query,
    flags,
    peak,
    total,
    out_stage,
    flag_recv,
    flag_send,
    deal_recv,
    query_recv,
    deal_send,
    chain_recv,
    chain_send,
    extra_recv,
    extra_send,
    out_recv,
    out_send,
):
    R = rows_of_tiles
    planes = frames // WT
    layers = planes // R
    rows = queries.shape[0]
    tile = rows * parts
    halves = parts // (2 * CORES)
    groups = WT * halves
    far = R + 1

    frame = lax.axis_index("frame")
    part = lax.axis_index("head")
    z, x = frame // WT, frame % WT
    layer, row = z // R, z % R
    y, k = part // CORES, part % CORES
    pair_half, p = y // 2, y % 2
    group = x * halves + pair_half
    inner, outer = 1 - k, k

    def reach(source, way):
        its_layer, its_row = source // R, source % R
        if way == 0:
            more_layers, more_rows = its_layer < layers - 1, its_row < R - 1
        else:
            more_layers, more_rows = its_layer > 0, its_row > 0
        rows_on = jnp.where(more_rows, 1, 0)
        return jnp.where(more_layers, R + rows_on, rows_on)

    def source_of(d, way):
        return z - d if way == 0 else z + d

    def travels(d, way, hop):
        source = source_of(d, way)
        inside = (source >= 0) & (source < planes)
        return inside & (hop <= reach(jnp.clip(source, 0, planes - 1), way))

    def steps_to(d, way):
        layer_step = jnp.where(d >= R - 1, -1, 0)
        row_step = jnp.where((d == 1) | (d == far), -1, jnp.where(d == R - 1, 1, 0))
        return (layer_step, row_step) if way == 0 else (-layer_step, -row_step)

    def used(d, way):
        layer_step, row_step = steps_to(d, way)
        there, its_row = layer + layer_step, row + row_step
        close = (d == 1) | (d >= R - 1)
        return close & (there >= 0) & (there < layers) & (its_row >= 0) & (its_row < R)

    def slot_of(d, way):
        return 1 + 2 * (d - 1) + way

    def column_of(unit):
        return jnp.where(unit == 2, 2 * p + k, 2 * k + unit)

    def head_of(unit):
        return 3 * group + jnp.where(unit == 2, 1, 2 * p)

    def lanes(index):
        return pl.ds(pl.multiple_of(index * HEAD_DIM, HEAD_DIM), HEAD_DIM)

    def own_rows(index):
        return pl.ds(pl.multiple_of(index * rows, rows), rows)

    def send_or_copy(mine, src, dst, send_sem, recv_sem, target):
        @pl.when(mine)
        def _():
            pltpu.make_async_copy(src, dst, recv_sem).start()

        @pl.when(jnp.logical_not(mine))
        def _():
            pltpu.make_async_remote_copy(
                src, dst, send_sem, recv_sem, device_id=target, device_id_type=MESH
            ).start()

    def await_bytes(ref, sem):
        pltpu.make_async_copy(ref, ref, sem).wait()

    barrier = pltpu.get_barrier_semaphore()
    plane_size = WT * parts

    def greet(i, carry):
        other_x = (x + i // parts) % WT
        other_part = (part + i % parts) % parts
        pl.semaphore_signal(
            barrier, inc=1, device_id=(z * WT + other_x, other_part), device_id_type=MESH
        )
        return carry

    lax.fori_loop(1, plane_size, greet, 0)

    @pl.when(z > 0)
    def _():
        pl.semaphore_signal(barrier, inc=1, device_id=(frame - WT, part), device_id_type=MESH)

    @pl.when(z < planes - 1)
    def _():
        pl.semaphore_signal(barrier, inc=1, device_id=(frame + WT, part), device_id_type=MESH)

    places = lax.broadcasted_iota(jnp.int32, (FLAG_ROWS, HEAD_DIM), 0)
    live_count = counts[0]

    def mark(j, live):
        listed = windows[0, j]
        place = (
            (listed // (R * WT) - layer + 1) * 9
            + (listed % (R * WT) // WT - row + 1) * 3
            + (listed % WT - x + 1)
        )
        place = jnp.where(j < live_count, place, FLAG_ROWS)
        return jnp.where(places == place, jnp.float32(1), live)

    flags[x] = lax.fori_loop(
        0, windows.shape[1], mark, jnp.zeros((FLAG_ROWS, HEAD_DIM), jnp.float32)
    )
    peak[...] = jnp.full(peak.shape, LOW, jnp.float32)
    total[...] = jnp.zeros(total.shape, jnp.float32)

    greeted = plane_size - 1 + jnp.where(z > 0, 1, 0) + jnp.where(z < planes - 1, 1, 0)
    pl.semaphore_wait(barrier, greeted)

    def dealt(head):
        if head == 1:
            return x // 2, x % 2, 2
        return head // 2, x // 2, x % 2

    def deal(head, tensors):
        to_p, to_core, unit = dealt(head)

        def one(i, carry):
            other = (group + i) % groups
            other_x, other_half = other // halves, other % halves
            other_part = (other_half * 2 + to_p) * CORES + to_core
            mine = (other == group) & (to_p == p) & (to_core == k)
            target = (z * WT + other_x, other_part)
            column = lanes(3 * other + head)
            for tensor in tensors:
                if tensor == 0:
                    src, dst, sem = keys, kv.at[0, unit, 0], deal_recv.at[unit]
                elif tensor == 1:
                    src, dst, sem = values, value_stage.at[unit], deal_recv.at[unit]
                else:
                    src, dst, sem = queries, query.at[unit], query_recv
                send_or_copy(
                    mine,
                    src.at[:, column],
                    dst.at[own_rows(part)],
                    deal_send.at[tensor, head],
                    sem,
                    target,
                )
            return carry

        lax.fori_loop(0, groups, one, 0)

    for head in (1, 0, 2):
        deal(head, (0, 1))
    for i in range(1, WT):
        pltpu.make_async_remote_copy(
            flags.at[x],
            flags.at[x],
            flag_send.at[i - 1],
            flag_recv.at[i - 1],
            device_id=(z * WT + (x + i) % WT, part),
            device_id_type=MESH,
        ).start()
    for head in (1, 0, 2):
        deal(head, (2,))

    def chain(d, way, unit):
        slot = jnp.where(d == 0, 0, slot_of(d, way))
        target = (frame + (WT if way == 0 else frames - WT)) % frames
        return pltpu.make_async_remote_copy(
            kv.at[slot, unit],
            kv.at[slot_of(d + 1, way), unit],
            chain_send.at[way, d, unit],
            chain_recv.at[way, d, unit],
            device_id=(target, part),
            device_id_type=MESH,
        )

    across = part + 1 - 2 * k
    has_partner = p != k
    partner = (pair_half * 2 + (1 - p)) * CORES + (1 - k)

    def extra(slot, which):
        unit = inner if which == 0 else 2
        return pltpu.make_async_remote_copy(
            kv.at[slot, unit],
            kv.at[slot, 3 + which],
            extra_send.at[slot, which],
            extra_recv.at[slot, which],
            device_id=(frame, partner if which == 2 else across),
            device_id_type=MESH,
        )

    def start_extras(slot, s):
        @pl.when(s == 0)
        def _():
            extra(slot, 1).start()

            @pl.when(has_partner)
            def _():
                extra(slot, 2).start()

        @pl.when(s == 1)
        def _():
            extra(slot, 0).start()

    def await_extras(slot, s):
        @pl.when(s == 1)
        def _():
            extra(slot, 1).wait_recv()

            @pl.when(has_partner)
            def _():
                extra(slot, 2).wait_recv()

        @pl.when(s == 2)
        def _():
            extra(slot, 0).wait_recv()

    def unit_at(s):
        return jnp.where(s == 0, 2, jnp.where(s == 1, inner, outer))

    def launch(s, carry):
        unit = unit_at(s)
        await_bytes(kv.at[0, unit], deal_recv.at[unit])
        for block in range(tile // HEAD_DIM):
            span = pl.ds(block * HEAD_DIM, HEAD_DIM)
            kv[0, unit, 1, span, :] = value_stage[unit, span, :].T
        for way in range(2):

            @pl.when(travels(0, way, 1))
            def _():
                chain(0, way, unit).start()

        start_extras(0, s)
        return carry

    lax.fori_loop(0, 3, launch, 0)
    await_bytes(query, query_recv)
    for i in range(1, WT):
        pltpu.make_async_remote_copy(
            flags.at[x],
            flags.at[(x - i) % WT],
            flag_send.at[i - 1],
            flag_recv.at[i - 1],
            device_id=(z * WT + (x + i) % WT, part),
            device_id_type=MESH,
        ).wait()

    beside = 1 - 2 * k
    summed = jnp.ones((SUM_ROWS, tile), jnp.bfloat16)

    def attend(i, d):
        on_q = jnp.where(
            (i == 0) | (i == 3) | (i == 4), 2, jnp.where((i == 2) | (i == 5), outer, inner)
        )
        on_kv = jnp.where(
            i <= 2,
            jnp.where(i == 0, 2, inner),
            jnp.where(
                i <= 4,
                jnp.where(i == 3, 4, jnp.where(has_partner, 5, 2)),
                jnp.where(i == 7, 3, outer),
            ),
        )
        shift = jnp.where(
            (i == 2) | (i == 3) | (i == 7), beside, jnp.where((i == 4) | (i == 6), -beside, 0)
        )
        column = column_of(on_q)
        one_query = query[on_q]

        def side(way):
            layer_step, row_step = steps_to(d, way)
            place = (layer_step + 1) * 9 + (row_step + 1) * 3 + shift + 1
            if way == 1:
                place = jnp.where(d == 0, FLAG_ROWS - 1, place)
            slot = jnp.where(used(d, way), slot_of(d, way), 0)
            flag = flags[column, pl.ds(place, 1), :]
            live = jnp.concatenate([flag] * (tile // HEAD_DIM), axis=1) > 0.5
            scores = lax.dot_general(
                kv[slot, on_kv, 0],
                one_query,
                (((1,), (1,)), ((), ())),
                preferred_element_type=jnp.float32,
            )
            top = jnp.where(live, jnp.max(scores, axis=0, keepdims=True), LOW)
            turned = kv[slot, on_kv, 1]
            turned = jnp.concatenate(
                [turned[b * HEAD_DIM : (b + 1) * HEAD_DIM] for b in range(tile // HEAD_DIM)], axis=1
            )
            return live, scores, top, jnp.concatenate([turned, summed], axis=0)

        sides = [side(0), side(1)]
        before = peak[on_q]
        now = jnp.maximum(before, jnp.maximum(sides[0][2], sides[1][2]))
        result = total[on_q] * jnp.exp2((before - now) * EXPONENT_SCALE)
        for live, scores, _, turned in sides:
            base = jnp.where(live, now, -LOW)
            weights = jnp.exp2((scores - base) * EXPONENT_SCALE).astype(jnp.bfloat16)
            result += jnp.dot(turned, weights, preferred_element_type=jnp.float32)
        peak[on_q] = now
        total[on_q] = result

    def step(t, carry):
        d, s = t // 3, t % 3
        unit = unit_at(s)

        @pl.when(d > 0)
        def _():
            for way in range(2):

                @pl.when(travels(d, way, d))
                def _():
                    chain(d - 1, way, unit).wait_recv()

                    @pl.when(travels(d, way, d + 1))
                    def _():
                        chain(d, way, unit).start()

                @pl.when(used(d, way))
                def _():
                    start_extras(slot_of(d, way), s)

        @pl.when(d == 0)
        def _():
            await_extras(0, s)

        @pl.when(d > 0)
        def _():
            for way in range(2):

                @pl.when(used(d, way))
                def _():
                    await_extras(slot_of(d, way), s)

        close = (d <= 1) | (d >= R - 1)
        first = jnp.where(s == 0, 0, jnp.where(s == 1, 1, 5))
        last = jnp.where(s == 0, 1, jnp.where(s == 1, 5, 8))

        def one(i, carry):
            attend(i, d)
            return carry

        lax.fori_loop(first, jnp.where(close, last, first), one, 0)
        return carry

    lax.fori_loop(0, 3 * (far + 1), step, 0)

    def deliver(s, carry):
        unit = unit_at(s)
        column = column_of(unit)
        sums = total[unit]
        scaled = sums[:HEAD_DIM] * (1.0 / sums[HEAD_DIM : HEAD_DIM + 1])
        out_stage[unit] = scaled.T.astype(jnp.bfloat16)

        def one(i, carry):
            to = (part + i) % parts
            send_or_copy(
                (to == part) & (column == x),
                out_stage.at[unit, own_rows(to)],
                out.at[:, lanes(head_of(unit))],
                out_send.at[unit],
                out_recv,
                (z * WT + column, to),
            )
            return carry

        lax.fori_loop(0, parts, one, 0)
        return carry

    lax.fori_loop(0, 3, deliver, 0)

    def settle_chain(t, carry):
        d, unit = t // 3, t % 3
        for way in range(2):

            @pl.when(travels(d, way, d + 1))
            def _():
                chain(d, way, unit).wait_send()

        return carry

    lax.fori_loop(0, 3 * far, settle_chain, 0)

    def settle_extras(slot):
        extra(slot, 0).wait_send()
        extra(slot, 1).wait_send()

        @pl.when(has_partner)
        def _():
            extra(slot, 2).wait_send()

    settle_extras(0)

    def settle(d, carry):
        for way in range(2):

            @pl.when(used(d, way))
            def _():
                settle_extras(slot_of(d, way))

        return carry

    lax.fori_loop(1, far + 1, settle, 0)

    def settle_sends(some_mine, count, sem):
        @pl.when(some_mine)
        def _():
            await_bytes(query.at[0, pl.ds(0, (count - 1) * rows)], sem)

        @pl.when(jnp.logical_not(some_mine))
        def _():
            await_bytes(query.at[0, pl.ds(0, count * rows)], sem)

    for head in range(3):
        to_p, to_core, _ = dealt(head)
        for tensor in range(3):
            settle_sends((to_p == p) & (to_core == k), groups, deal_send.at[tensor, head])
    for unit in range(3):
        settle_sends(column_of(unit) == x, parts, out_send.at[unit])
    await_bytes(out, out_recv)


def attention(rows_of_tiles, frames, parts, queries, keys, values, windows, counts):
    rows, width = queries.shape
    tile = rows * parts
    far = rows_of_tiles + 1
    slots = 1 + 2 * far
    any_space = pl.BlockSpec(memory_space=pl.ANY)
    scalars = pl.BlockSpec(memory_space=pltpu.SMEM)
    dma = pltpu.SemaphoreType.DMA
    return pl.pallas_call(
        functools.partial(kernel, rows_of_tiles, frames, parts),
        out_shape=jax.ShapeDtypeStruct((rows, width), jnp.bfloat16),
        in_specs=[scalars, scalars, any_space, any_space, any_space],
        out_specs=any_space,
        scratch_shapes=[
            pltpu.VMEM((slots, 6, 2, tile, HEAD_DIM), jnp.bfloat16),
            pltpu.VMEM((3, tile, HEAD_DIM), jnp.bfloat16),
            pltpu.VMEM((3, tile, HEAD_DIM), jnp.bfloat16),
            pltpu.VMEM((WT, FLAG_ROWS, HEAD_DIM), jnp.float32),
            pltpu.VMEM((3, 1, tile), jnp.float32),
            pltpu.VMEM((3, HEAD_DIM + SUM_ROWS, tile), jnp.float32),
            pltpu.VMEM((3, tile, HEAD_DIM), jnp.bfloat16),
            dma((WT - 1,)),
            dma((WT - 1,)),
            dma((3,)),
            dma,
            dma((3, 3)),
            dma((2, far, 3)),
            dma((2, far, 3)),
            dma((slots, 3)),
            dma((slots, 3)),
            dma,
            dma((3,)),
        ],
        compiler_params=pltpu.CompilerParams(
            collective_id=0, has_side_effects=True, vmem_limit_bytes=48 * 1024 * 1024
        ),
    )(windows, counts, queries, keys, values)


def solution(mesh):
    split = P(("frame", "head"), None)
    return jax.shard_map(
        functools.partial(attention, HT, mesh.shape["frame"], mesh.shape["head"]),
        mesh=mesh,
        in_specs=(split, split, split, P("frame", None), P("frame")),
        out_specs=split,
        check_vma=False,
    )
```

time: 1290 us -> 97.6 us (0.08)
  the two profiles are of different devices: /device:TPU:103 before, /device:TPU:321 now
where the time goes in v1:
time: 97.6 us; the launch traced here: 97.3 us
  Pallas kernels  93 us (95%)
  local copies, waits for them, and re-layouts  3.6 us (4%)
    pallas_call x1, Pallas kernels, attention(): pl.pallas_call(functools.partial(kernel, rows_of_tiles, frames, parts), o...  93 us
    unnamed x9, local copies, waits for them, and re-layouts  3.6 us

profile of v1, /device:TPU:321, one launch (start us, length us, event | category | flops | bytes accessed | tf_op | source)
XLA Modules:
  0.0 97.3 jit_solution(7397401689145452462)
XLA Ops:
  0.0 0.0 copy-start.3
  0.7 0.0 copy-done.3
  0.7 0.0 copy-start
  0.7 1.0 copy-done
  1.6 0.0 copy-start.1
  1.6 1.0 copy-done.1
  2.6 0.0 copy-start.2
  2.6 1.0 copy-done.2
  3.6 93.0 %shard_map.55 = bf16[48,3072]{1,0:T(8,128)(2,1)S(1)} custom-call(s32[1,27]{1,0:T(1,128)S(1)} %copy-done.3, s32[1]{0:T(128)S(6)} %copy.7.counts, bf16[48,3072]{1,0:T(8,128)(2,1)S(1)} %copy-done, bf16[48,3072]{1,0:T(8,128)(2,1)S(1)} %copy-done.1, bf16[48,3072]{1,0:T(8,128)(2,1)S(1)} %copy-done.2), custom_call_target="tpu_custom_call" | custom-call | tf_op jit(solution)/shard_map/pallas_call | solution.py:481
  96.6 0.7 copy.8
Async XLA Ops:
  0.0 0.7 copy-start.3
  0.7 1.0 copy-start
  1.6 1.0 copy-start.1
  2.6 1.0 copy-start.2

commit v2 on v1

v2 whole, which is shorter than its diff:
```python
import functools

import jax
import jax.numpy as jnp
from jax import lax
from jax.experimental import pallas as pl
from jax.experimental.pallas import tpu as pltpu
from jax.sharding import PartitionSpec as P

HEAD_DIM = 128
HT = 4
WT = 4
CORES = 2
FLAG_ROWS = 32
WINDOW = 27
SUM_ROWS = 16
LOW = -3.0e38
EXPONENT_SCALE = HEAD_DIM ** (-0.5) * 1.4426950408889634
MESH = pl.DeviceIdType.MESH


def kernel(
    rows_of_tiles,
    frames,
    parts,
    windows,
    counts,
    queries,
    keys,
    values,
    out,
    listed,
    live_count,
    kv,
    raw_keys,
    value_stage,
    query,
    flags,
    peak,
    total,
    out_stage,
    list_sem,
    flag_recv,
    flag_send,
    raw_recv,
    raw_send,
    key_recv,
    key_send,
    value_recv,
    value_send,
    query_recv,
    query_send,
    chain_recv,
    chain_send,
    extra_recv,
    extra_send,
    out_recv,
    out_send,
):
    R = rows_of_tiles
    planes = frames // WT
    layers = planes // R
    rows = queries.shape[0]
    tile = rows * parts
    blocks = tile // HEAD_DIM
    halves = parts // (2 * CORES)
    far = R + 1

    frame = lax.axis_index("frame")
    part = lax.axis_index("head")
    z, x = frame // WT, frame % WT
    layer, row = z // R, z % R
    y, k = part // CORES, part % CORES
    half, p = y // 2, y % 2
    inner, outer = 1 - k, k
    corner = z * WT

    def turned_by(index, by, size):
        moved = index + by
        return jnp.where(moved >= size, moved - size, moved)

    def loop(first, last, body):
        def one(i, carry):
            body(i)
            return carry

        lax.fori_loop(first, last, one, 0)

    lists = [
        pltpu.make_async_copy(windows, listed, list_sem.at[0]),
        pltpu.make_async_copy(counts, live_count, list_sem.at[1]),
    ]
    for copy in lists:
        copy.start()

    barrier = pltpu.get_barrier_semaphore()

    def greet(to):
        pl.semaphore_signal(barrier, inc=1, device_id=to, device_id_type=MESH)

    @pl.when(z > 0)
    def _():
        greet((frame - WT, part))

    @pl.when(z < planes - 1)
    def _():
        greet((frame + WT, part))

    other_parts = [turned_by(part, j, parts) if j else part for j in range(parts)]

    def greet_column(i):
        to = corner + turned_by(x, i, WT)
        for other in other_parts:
            greet((to, other))

    for other in other_parts[1:]:
        greet((frame, other))
    loop(1, WT, greet_column)
    greeted = WT * parts - 1 + jnp.where(z > 0, 1, 0) + jnp.where(z < planes - 1, 1, 0)
    pl.semaphore_wait(barrier, greeted)

    seen = [(z, layer, row), (planes - 1 - z, layers - 1 - layer, R - 1 - row)]

    def travels(d, way, hop):
        source = seen[way][0] - d
        its_row = seen[way][2] - d
        its_row = jnp.where(its_row < 0, its_row + R, its_row)
        its_row = jnp.where(its_row < 0, its_row + R, its_row)
        rows_on = its_row < R - 1
        far_enough = (hop <= R) | ((hop == far) & rows_on)
        short = (hop == 1) & rows_on
        more_layers = source < planes - R
        return (source >= 0) & ((more_layers & far_enough) | (jnp.logical_not(more_layers) & short))

    def steps_to(d, way):
        sign = 2 * way - 1
        row_step = jnp.where((d == 1) | (d == far), 1, jnp.where(d == R - 1, -1, 0))
        return sign * jnp.where(d >= R - 1, 1, 0), sign * row_step

    def used(d, way):
        _, its_layer, its_row = seen[way]
        near = (d == 1) & (its_row >= 1)
        back = (d == R - 1) & (its_row < R - 1)
        over = (d == R) | ((d == far) & (its_row >= 1))
        return near | ((its_layer >= 1) & (back | over))

    def slot_of(d, way):
        return 1 + 2 * (d - 1) + way

    def column_of(unit):
        return jnp.where(unit == 2, 2 * p + k, 2 * k + unit)

    def head_of(unit):
        return 3 * (x * halves + half) + jnp.where(unit == 2, 1, 2 * p)

    def lanes(index):
        return pl.ds(pl.multiple_of(index * HEAD_DIM, HEAD_DIM), HEAD_DIM)

    def own_rows(index):
        return pl.ds(pl.multiple_of(index * rows, rows), rows)

    def send(src, dst, send_sem, recv_sem, target):
        pltpu.make_async_remote_copy(
            src, dst, send_sem, recv_sem, device_id=target, device_id_type=MESH
        ).start()

    def send_or_copy(mine, src, dst, send_sem, recv_sem, target):
        @pl.when(mine)
        def _():
            pltpu.make_async_copy(src, dst, recv_sem).start()

        @pl.when(jnp.logical_not(mine))
        def _():
            send(src, dst, send_sem, recv_sem, target)

    def await_bytes(ref, sem):
        pltpu.make_async_copy(ref, ref, sem).wait()

    piece = halves * 3 * HEAD_DIM
    above = jnp.where(z == planes - 1, x, frame + WT)
    below = jnp.where(z == 0, frame + (frames - WT), frame - WT)

    def raw(way, i):
        columns = pl.ds(pl.multiple_of(turned_by(x, i, WT) * piece, HEAD_DIM), piece)
        return pltpu.make_async_remote_copy(
            keys.at[:, columns],
            raw_keys.at[way, :, columns],
            raw_send.at[way, i],
            raw_recv.at[way, i],
            device_id=(jnp.where(way == 0, above, below), part),
            device_id_type=MESH,
        )

    def start_raw(i):
        for way in range(2):

            @pl.when(travels(0, way, 1))
            def _():
                raw(way, i).start()

    loop(0, WT, start_raw)

    routes = [(0, x // 2, x % 2), (x // 2, x % 2, 2), (1, x // 2, x % 2)]
    mine = [(to_p == p) & (to_core == k) for to_p, to_core, _ in routes]
    mine_rows = own_rows(part)

    def deal_head(at, head, src, dst_of, send_sem_of, recv_sem_of):
        to_p, to_core, unit = routes[head]
        to_x = turned_by(x, at, WT)
        dst = dst_of(unit).at[mine_rows]
        first = 3 * halves * to_x + head
        for j in range(halves):
            other_half = turned_by(half, j, halves) if j else half
            copy = (
                src.at[:, lanes(first + 3 * other_half)],
                dst,
                send_sem_of(head),
                recv_sem_of(unit),
                (corner + to_x, (other_half * 2 + to_p) * CORES + to_core),
            )
            if j == 0:
                send_or_copy((at == 0) & mine[head], *copy)
            else:
                send(*copy)

    def deal(*how):
        for head in (1, 0, 2):
            loop(0, WT, lambda at: deal_head(at, head, *how))

    deal(values, value_stage.at.__getitem__, value_send.at.__getitem__, value_recv.at.__getitem__)

    def chain(d, way, unit, which):
        slot = jnp.where(d == 0, 0, slot_of(d, way))
        return pltpu.make_async_remote_copy(
            kv.at[slot, unit, which],
            kv.at[slot_of(d + 1, way), unit, which],
            chain_send.at[way, d, unit, which],
            chain_recv.at[way, d, unit, which],
            device_id=(jnp.where(way == 0, above, below), part),
            device_id_type=MESH,
        )

    across = part + 1 - 2 * k
    has_partner = p != k
    partner = (half * 2 + (1 - p)) * CORES + (1 - k)

    def extra(slot, which):
        unit = inner if which == 0 else 2
        return pltpu.make_async_remote_copy(
            kv.at[slot, unit],
            kv.at[slot, 3 + which],
            extra_send.at[slot, which],
            extra_recv.at[slot, which],
            device_id=(frame, partner if which == 2 else across),
            device_id_type=MESH,
        )

    def start_extras(slot, s):
        @pl.when(s == 0)
        def _():
            extra(slot, 1).start()

            @pl.when(has_partner)
            def _():
                extra(slot, 2).start()

        @pl.when(s == 1)
        def _():
            extra(slot, 0).start()

    def unit_at(s):
        return jnp.where(s == 0, 2, jnp.where(s == 1, inner, outer))

    def launch(s):
        unit = unit_at(s)
        await_bytes(value_stage.at[unit], value_recv.at[unit])

        def turn(block):
            span = pl.ds(pl.multiple_of(block * HEAD_DIM, HEAD_DIM), HEAD_DIM)
            kv[0, unit, 1, span, :] = value_stage[unit, span, :].T

        loop(0, blocks, turn)

        for way in range(2):

            @pl.when(travels(0, way, 1))
            def _():
                chain(0, way, unit, 1).start()

    def deal_piece(i):
        for way in range(2):

            @pl.when(travels(1, way, 1))
            def _():
                raw(way, i).wait_recv()
                for head in (1, 0, 2):
                    deal_head(
                        i,
                        head,
                        raw_keys.at[way],
                        lambda unit: kv.at[1 + way, unit, 0],
                        lambda head: key_send.at[1 + way, head],
                        lambda unit: key_recv.at[1 + way, unit],
                    )

        @pl.when(i < 3)
        def _():
            launch(i)

    loop(0, WT, deal_piece)

    for copy in lists:
        copy.wait()
    place = lax.broadcasted_iota(jnp.int32, (FLAG_ROWS, WINDOW), 0)
    layer_place = jnp.where(place >= 18, 2, jnp.where(place >= 9, 1, 0))
    rest = place - 9 * layer_place
    row_place = jnp.where(rest >= 6, 2, jnp.where(rest >= 3, 1, 0))
    rest = rest - 3 * row_place
    named = ((layer + layer_place - 1) * R + row + row_place - 1) * WT + x + rest - 1
    entry = lax.broadcasted_iota(jnp.int32, (FLAG_ROWS, WINDOW), 1)
    found = (named == listed[...]) & (entry < live_count[...]) & (place < WINDOW)
    found = jnp.max(jnp.where(found, jnp.float32(1), jnp.float32(0)), axis=1, keepdims=True)
    flags[x] = jnp.broadcast_to(found, (FLAG_ROWS, HEAD_DIM))

    def flag_copy(i, landing):
        return pltpu.make_async_remote_copy(
            flags.at[x],
            flags.at[landing],
            flag_send.at[i - 1],
            flag_recv.at[i - 1],
            device_id=(corner + turned_by(x, i, WT), part),
            device_id_type=MESH,
        )

    loop(1, WT, lambda i: flag_copy(i, x).start())

    def pass_keys(s):
        unit = unit_at(s)
        for way in range(2):

            @pl.when(travels(1, way, 1))
            def _():
                await_bytes(kv.at[1 + way, unit, 0], key_recv.at[1 + way, unit])

            @pl.when(travels(1, way, 2))
            def _():
                chain(1, way, unit, 0).start()

    def pass_values(s):
        unit = unit_at(s)
        for way in range(2):

            @pl.when(travels(1, way, 1))
            def _():
                chain(0, way, unit, 1).wait_recv()

            @pl.when(travels(1, way, 2))
            def _():
                chain(1, way, unit, 1).start()

            @pl.when(used(1, way))
            def _():
                start_extras(slot_of(1, way), s)

    loop(0, 3, pass_keys)
    loop(0, 3, pass_values)
    deal(queries, query.at.__getitem__, query_send.at.__getitem__, lambda unit: query_recv)
    deal(
        keys,
        lambda unit: kv.at[0, unit, 0],
        lambda head: key_send.at[0, head],
        lambda unit: key_recv.at[0, unit],
    )

    def clear(unit):
        peak[unit] = jnp.full(peak.shape[1:], LOW, jnp.float32)

        def clear_rows(i):
            span = pl.ds(pl.multiple_of(i * SUM_ROWS, SUM_ROWS), SUM_ROWS)
            total[unit, span, :] = jnp.zeros((SUM_ROWS, tile), jnp.float32)

        loop(0, HEAD_DIM // SUM_ROWS + 1, clear_rows)

    loop(0, 3, clear)
    loop(1, WT, lambda i: flag_copy(i, turned_by(x, WT - i, WT)).wait())

    beside = 1 - 2 * k
    summed = jnp.ones((SUM_ROWS, tile), jnp.bfloat16)

    def attend(i, d):
        on_q = jnp.where((i == 0) | (i == 3) | (i == 4), 2, jnp.where((i == 2) | (i == 6), outer, inner))
        on_kv = jnp.where(
            i <= 2,
            jnp.where(i == 0, 2, inner),
            jnp.where(
                i <= 4,
                jnp.where(i == 3, 4, jnp.where(has_partner, 5, 2)),
                jnp.where(i == 5, 3, outer),
            ),
        )
        shift = jnp.where(
            (i == 2) | (i == 3) | (i == 5), beside, jnp.where((i == 4) | (i == 7), -beside, 0)
        )
        column = column_of(on_q)
        one_query = query[on_q]

        def side(way):
            layer_step, row_step = steps_to(d, way)
            place = (layer_step + 1) * 9 + (row_step + 1) * 3 + shift + 1
            if way == 1:
                place = jnp.where(d == 0, FLAG_ROWS - 1, place)
            there = used(d, way)
            slot = jnp.where(there, slot_of(d, way), 0)
            at = jnp.where(there | (d == 0), on_kv, jnp.minimum(on_kv, 2))
            flag = flags[column, pl.ds(place, 1), :]
            live = jnp.concatenate([flag] * blocks, axis=1) > 0.5
            scores = lax.dot_general(
                kv[slot, at, 0],
                one_query,
                (((1,), (1,)), ((), ())),
                preferred_element_type=jnp.float32,
            )
            top = jnp.where(live, jnp.max(scores, axis=0, keepdims=True), LOW)
            turned = kv[slot, at, 1]
            turned = jnp.concatenate(
                [turned[b * HEAD_DIM : (b + 1) * HEAD_DIM] for b in range(blocks)], axis=1
            )
            return live, scores, top, jnp.concatenate([turned, summed], axis=0)

        sides = [side(0), side(1)]
        before = peak[on_q]
        now = jnp.maximum(before, jnp.maximum(sides[0][2], sides[1][2]))
        result = total[on_q] * jnp.exp2((before - now) * EXPONENT_SCALE)
        for live, scores, _, turned in sides:
            base = jnp.where(live, now, -LOW)
            weights = jnp.exp2((scores - base) * EXPONENT_SCALE).astype(jnp.bfloat16)
            result += jnp.dot(turned, weights, preferred_element_type=jnp.float32)
        peak[on_q] = now
        total[on_q] = result

    def deliver(unit):
        column = column_of(unit)
        sums = total[unit]
        scaled = sums[:HEAD_DIM] * (1.0 / sums[HEAD_DIM : HEAD_DIM + 1])
        out_stage[unit] = scaled.T.astype(jnp.bfloat16)

        target = corner + column
        head_lanes = lanes(head_of(unit))
        for i in range(parts):
            to = turned_by(part, i, parts) if i else part
            copy = (
                out_stage.at[unit, own_rows(to)],
                out.at[:, head_lanes],
                out_send.at[unit],
                out_recv,
                (target, to),
            )
            if i == 0:
                send_or_copy(column == x, *copy)
            else:
                send(*copy)

    def settle_chain(d, unit):
        for way in range(2):

            @pl.when(travels(d, way, d + 1))
            def _():
                @pl.when(d > 0)
                def _():
                    chain(d, way, unit, 0).wait_send()

                chain(d, way, unit, 1).wait_send()

    def settle_extras(slot, s):
        @pl.when(s == 0)
        def _():
            extra(slot, 1).wait_send()

            @pl.when(has_partner)
            def _():
                extra(slot, 2).wait_send()

        @pl.when(s == 1)
        def _():
            extra(slot, 0).wait_send()

    def settle_sends(some_mine, sem):
        @pl.when(some_mine)
        def _():
            await_bytes(query.at[0, pl.ds(0, tile - rows)], sem)

        @pl.when(jnp.logical_not(some_mine))
        def _():
            await_bytes(query.at[0], sem)

    def settle_deals():
        def settle_raw(i):
            for way in range(2):

                @pl.when(travels(0, way, 1))
                def _():
                    raw(way, i).wait_send()

        loop(0, WT, settle_raw)
        for head in range(3):
            settle_sends(mine[head], query_send.at[head])
            settle_sends(mine[head], value_send.at[head])
            settle_sends(mine[head], key_send.at[0, head])
            for way in range(2):

                @pl.when(travels(1, way, 1))
                def _():
                    settle_sends(mine[head], key_send.at[1 + way, head])

    def work(plane, s):
        def await_extra(which):
            @pl.when(plane == 0)
            def _():
                extra(0, which).wait_recv()

            for way in range(2):

                @pl.when(used(plane, way))
                def _():
                    extra(slot_of(plane, way), which).wait_recv()

        def one(i):
            @pl.when(i == 3)
            def _():
                await_extra(1)

                @pl.when(has_partner)
                def _():
                    await_extra(2)

            @pl.when(i == 5)
            def _():
                await_extra(0)

            attend(i, plane)

            @pl.when((plane == far) & ((i == 4) | (i >= 6)))
            def _():
                deliver(jnp.where(i == 4, 2, jnp.where(i == 6, outer, inner)))

        loop(jnp.where(s == 0, 0, jnp.where(s == 1, 1, 5)), jnp.where(s == 0, 1, jnp.where(s == 1, 5, 8)), one)

    def step(d, s):
        unit = unit_at(s)
        for way in range(2):
            on = travels(d, way, d + 1)

            @pl.when(travels(d, way, d))
            def _():
                for which in range(2):
                    chain(d - 1, way, unit, which).wait_recv()

                    @pl.when(on)
                    def _():
                        chain(d, way, unit, which).start()

            @pl.when(used(d, way))
            def _():
                start_extras(slot_of(d, way), s)

        settle_chain(d - 2, unit)

        @pl.when(d == 2)
        def _():
            @pl.when(s == 0)
            def _():
                await_bytes(query, query_recv)

            await_bytes(kv.at[0, unit, 0], key_recv.at[0, unit])
            start_extras(0, s)

        @pl.when(d == R)
        def _():
            settle_extras(0, s)

            @pl.when(s == 0)
            def _():
                settle_deals()

        for way in range(2):

            @pl.when(used(d - 1, way))
            def _():
                settle_extras(slot_of(d - 1, way), s)

        def turn(i):
            work(jnp.where(d == 2, 1, jnp.where((d == 3) & (i == 0), 0, d)), s)

        loop(0, jnp.where(d == 3, 2, 1), turn)

    def hop(d):
        loop(0, 3, lambda s: step(d, s))

    loop(2, far + 1, hop)

    def settle_last(s):
        settle_chain(far - 1, s)
        for way in range(2):

            @pl.when(used(far, way))
            def _():
                settle_extras(slot_of(far, way), s)

    loop(0, 3, settle_last)
    loop(0, 3, lambda unit: settle_sends(column_of(unit) == x, out_send.at[unit]))
    await_bytes(out, out_recv)


def attention(rows_of_tiles, frames, parts, queries, keys, values, windows, counts):
    rows, width = queries.shape
    tile = rows * parts
    far = rows_of_tiles + 1
    slots = 1 + 2 * far
    any_space = pl.BlockSpec(memory_space=pltpu.HBM)
    dma = pltpu.SemaphoreType.DMA
    return pl.pallas_call(
        functools.partial(kernel, rows_of_tiles, frames, parts),
        out_shape=pltpu.VMEM((rows, width), jnp.bfloat16),
        in_specs=[any_space] * 5,
        out_specs=pl.BlockSpec(memory_space=pltpu.VMEM),
        scratch_shapes=[
            pltpu.VMEM((1, WINDOW), jnp.int32),
            pltpu.VMEM((1, 1), jnp.int32),
            pltpu.VMEM((slots, 6, 2, tile, HEAD_DIM), jnp.bfloat16),
            pltpu.VMEM((2, rows, width), jnp.bfloat16),
            pltpu.VMEM((3, tile, HEAD_DIM), jnp.bfloat16),
            pltpu.VMEM((3, tile, HEAD_DIM), jnp.bfloat16),
            pltpu.VMEM((WT, FLAG_ROWS, HEAD_DIM), jnp.float32),
            pltpu.VMEM((3, 1, tile), jnp.float32),
            pltpu.VMEM((3, HEAD_DIM + SUM_ROWS, tile), jnp.float32),
            pltpu.VMEM((3, tile, HEAD_DIM), jnp.bfloat16),
            dma((2,)),
            dma((WT - 1,)),
            dma((WT - 1,)),
            dma((2, WT)),
            dma((2, WT)),
            dma((3, 3)),
            dma((3, 3)),
            dma((3,)),
            dma((3,)),
            dma,
            dma((3,)),
            dma((2, far, 3, 2)),
            dma((2, far, 3, 2)),
            dma((slots, 3)),
            dma((slots, 3)),
            dma,
            dma((3,)),
        ],
        compiler_params=pltpu.CompilerParams(
            collective_id=0, has_side_effects=True, vmem_limit_bytes=60 * 1024 * 1024
        ),
    )(windows, counts.reshape(1, 1), queries, keys, values)


def solution(mesh):
    split = P(("frame", "head"), None)
    return jax.shard_map(
        functools.partial(attention, HT, mesh.shape["frame"], mesh.shape["head"]),
        mesh=mesh,
        in_specs=(split, split, split, P("frame", None), P("frame")),
        out_specs=split,
        check_vma=False,
    )
```

time: 97.6 us -> 88.2 us (0.904)
  the two profiles are of different devices: /device:TPU:321 before, /device:TPU:195 now
where the time goes in v2:
time: 88.2 us; the launch traced here: 88.1 us
  Pallas kernels  86.7 us (98%)
    pallas_call x1, Pallas kernels, attention(): pl.pallas_call(functools.partial(kernel, rows_of_tiles, frames, parts), o...  86.7 us

profile of v2, /device:TPU:195, one launch (start us, length us, event | category | flops | bytes accessed | tf_op | source)
XLA Modules:
  0.0 88.1 jit_solution(17779037663332606861)
XLA Ops:
  0.7 86.7 %shard_map.55 = bf16[48,3072]{1,0:T(8,128)(2,1)S(1)} custom-call(s32[1,27]{1,0:T(1,128)} %windows.1, s32[1,1]{1,0:T(1,128)} %bitcast.1.counts, bf16[48,3072]{1,0:T(8,128)(2,1)} %queries.1, bf16[48,3072]{1,0:T(8,128)(2,1)} %keys.1, bf16[48,3072]{1,0:T(8,128)(2,1)} %values.1), custom_call_target="tpu_custom_call" | custom-call | tf_op jit(solution)/shard_map/pallas_call | solution.py:621
  87.4 0.7 copy.7

commit v3 on v2

--- a/solution.py
+++ b/solution.py
@@ -106,16 +106,21 @@
     def _():
         greet((frame + WT, part))
 
-    other_parts = [turned_by(part, j, parts) if j else part for j in range(parts)]
-
-    def greet_column(i):
-        to = corner + turned_by(x, i, WT)
+    def far_first(t, way=0):
+        beside = jnp.where((t == 1) == (way == 0), 1, 3)
+        return jnp.where(t == 0, 2, jnp.where(t == WT - 1, 0, beside))
+
+    part_steps = sorted(range(parts), key=lambda j: (-min(j, parts - j), j))
+    other_parts = [turned_by(part, j, parts) if j else part for j in part_steps]
+
+    def greet_column(t):
+        to = corner + turned_by(x, far_first(t), WT)
         for other in other_parts:
             greet((to, other))
 
-    for other in other_parts[1:]:
+    loop(0, WT - 1, greet_column)
+    for other in other_parts[:-1]:
         greet((frame, other))
-    loop(1, WT, greet_column)
     greeted = WT * parts - 1 + jnp.where(z > 0, 1, 0) + jnp.where(z < planes - 1, 1, 0)
     pl.semaphore_wait(barrier, greeted)
 
@@ -181,7 +186,9 @@
     below = jnp.where(z == 0, frame + (frames - WT), frame - WT)
 
     def raw(way, i):
-        columns = pl.ds(pl.multiple_of(turned_by(x, i, WT) * piece, HEAD_DIM), piece)
+        columns = pl.ds(
+            pl.multiple_of(turned_by(x, far_first(i, way), WT) * piece, HEAD_DIM), piece
+        )
         return pltpu.make_async_remote_copy(
             keys.at[:, columns],
             raw_keys.at[way, :, columns],
@@ -225,7 +232,7 @@
 
     def deal(*how):
         for head in (1, 0, 2):
-            loop(0, WT, lambda at: deal_head(at, head, *how))
+            loop(0, WT, lambda t: deal_head(far_first(t), head, *how))
 
     deal(values, value_stage.at.__getitem__, value_send.at.__getitem__, value_recv.at.__getitem__)
 
@@ -295,7 +302,7 @@
                 raw(way, i).wait_recv()
                 for head in (1, 0, 2):
                     deal_head(
-                        i,
+                        far_first(i, way),
                         head,
                         raw_keys.at[way],
                         lambda unit: kv.at[1 + way, unit, 0],
@@ -308,6 +315,36 @@
             launch(i)
 
     loop(0, WT, deal_piece)
+
+    def pass_keys(s):
+        unit = unit_at(s)
+        for way in range(2):
+
+            @pl.when(travels(1, way, 1))
+            def _():
+                await_bytes(kv.at[1 + way, unit, 0], key_recv.at[1 + way, unit])
+
+            @pl.when(travels(1, way, 2))
+            def _():
+                chain(1, way, unit, 0).start()
+
+    def pass_values(s):
+        unit = unit_at(s)
+        for way in range(2):
+
+            @pl.when(travels(1, way, 1))
+            def _():
+                chain(0, way, unit, 1).wait_recv()
+
+            @pl.when(travels(1, way, 2))
+            def _():
+                chain(1, way, unit, 1).start()
+
+            @pl.when(used(1, way))
+            def _():
+                start_extras(slot_of(1, way), s)
+
+    loop(0, 3, pass_keys)
 
     for copy in lists:
         copy.wait()
@@ -334,35 +371,6 @@
 
     loop(1, WT, lambda i: flag_copy(i, x).start())
 
-    def pass_keys(s):
-        unit = unit_at(s)
-        for way in range(2):
-
-            @pl.when(travels(1, way, 1))
-            def _():
-                await_bytes(kv.at[1 + way, unit, 0], key_recv.at[1 + way, unit])
-
-            @pl.when(travels(1, way, 2))
-            def _():
-                chain(1, way, unit, 0).start()
-
-    def pass_values(s):
-        unit = unit_at(s)
-        for way in range(2):
-
-            @pl.when(travels(1, way, 1))
-            def _():
-                chain(0, way, unit, 1).wait_recv()
-
-            @pl.when(travels(1, way, 2))
-            def _():
-                chain(1, way, unit, 1).start()
-
-            @pl.when(used(1, way))
-            def _():
-                start_extras(slot_of(1, way), s)
-
-    loop(0, 3, pass_keys)
     loop(0, 3, pass_values)
     deal(queries, query.at.__getitem__, query_send.at.__getitem__, lambda unit: query_recv)
     deal(
@@ -446,8 +454,7 @@
 
         target = corner + column
         head_lanes = lanes(head_of(unit))
-        for i in range(parts):
-            to = turned_by(part, i, parts) if i else part
+        for to in other_parts:
             copy = (
                 out_stage.at[unit, own_rows(to)],
                 out.at[:, head_lanes],
@@ -455,7 +462,7 @@
                 out_recv,
                 (target, to),
             )
-            if i == 0:
+            if to is part:
                 send_or_copy(column == x, *copy)
             else:
                 send(*copy)
@@ -512,7 +519,7 @@
                 def _():
                     settle_sends(mine[head], key_send.at[1 + way, head])
 
-    def work(plane, s):
+    def work(plane, place, idle):
         def await_extra(which):
             @pl.when(plane == 0)
             def _():
@@ -543,10 +550,11 @@
             def _():
                 deliver(jnp.where(i == 4, 2, jnp.where(i == 6, outer, inner)))
 
-        loop(jnp.where(s == 0, 0, jnp.where(s == 1, 1, 5)), jnp.where(s == 0, 1, jnp.where(s == 1, 5, 8)), one)
-
-    def step(d, s):
-        unit = unit_at(s)
+        first = jnp.where(place == 0, 0, jnp.where(place == 1, 1, place + 3))
+        last = jnp.where(place == 0, 1, jnp.where(place == 1, 5, 2 * place + 2))
+        loop(first, jnp.where(idle, first, last), one)
+
+    def arrive(d, s, unit):
         for way in range(2):
             on = travels(d, way, d + 1)
 
@@ -565,21 +573,12 @@
 
         settle_chain(d - 2, unit)
 
-        @pl.when(d == 2)
-        def _():
+        @pl.when(d == R)
+        def _():
+            settle_extras(0, s)
+
             @pl.when(s == 0)
             def _():
-                await_bytes(query, query_recv)
-
-            await_bytes(kv.at[0, unit, 0], key_recv.at[0, unit])
-            start_extras(0, s)
-
-        @pl.when(d == R)
-        def _():
-            settle_extras(0, s)
-
-            @pl.when(s == 0)
-            def _():
                 settle_deals()
 
         for way in range(2):
@@ -588,13 +587,31 @@
             def _():
                 settle_extras(slot_of(d - 1, way), s)
 
-        def turn(i):
-            work(jnp.where(d == 2, 1, jnp.where((d == 3) & (i == 0), 0, d)), s)
-
-        loop(0, jnp.where(d == 3, 2, 1), turn)
+    def step(d, place):
+        s = jnp.where(place == 3, 2, place)
+        unit = unit_at(s)
+
+        def phase(turn):
+            @pl.when((turn == 0) & (d == 2) & (place != 2))
+            def _():
+                @pl.when(s == 0)
+                def _():
+                    await_bytes(query, query_recv)
+
+                await_bytes(kv.at[0, unit, 0], key_recv.at[0, unit])
+                start_extras(0, s)
+
+            @pl.when((turn == 1) & (place != 2))
+            def _():
+                arrive(d, s, unit)
+
+            idle = ((turn == 0) & (d > 3)) | ((turn == 1) & (d == 2))
+            work(jnp.where(turn == 1, d, jnp.where(d == 2, 1, 0)), place, idle)
+
+        loop(0, 2, phase)
 
     def hop(d):
-        loop(0, 3, lambda s: step(d, s))
+        loop(0, 4, lambda place: step(d, place))
 
     loop(2, far + 1, hop)
 

time: 88.2 us -> 86.4 us (0.980)
  the two profiles are of different devices: /device:TPU:195 before, /device:TPU:129 now
where the time goes in v3:
time: 86.4 us; the launch traced here: 86.3 us
  Pallas kernels  84.9 us (98%)
    pallas_call x1, Pallas kernels, attention(): pl.pallas_call(functools.partial(kernel, rows_of_tiles, frames, parts), o...  84.9 us

profile of v3, /device:TPU:129, one launch (start us, length us, event | category | flops | bytes accessed | tf_op | source)
XLA Modules:
  0.0 86.3 jit_solution(637155700950273117)
XLA Ops:
  0.7 84.9 %shard_map.55 = bf16[48,3072]{1,0:T(8,128)(2,1)S(1)} custom-call(s32[1,27]{1,0:T(1,128)} %windows.1, s32[1,1]{1,0:T(1,128)} %bitcast.1.counts, bf16[48,3072]{1,0:T(8,128)(2,1)} %queries.1, bf16[48,3072]{1,0:T(8,128)(2,1)} %keys.1, bf16[48,3072]{1,0:T(8,128)(2,1)} %values.1), custom_call_target="tpu_custom_call" | custom-call | tf_op jit(solution)/shard_map/pallas_call | solution.py:638
  85.5 0.7 copy.7

commit v4 on v3

--- a/solution.py
+++ b/solution.py
@@ -395,7 +395,7 @@
     beside = 1 - 2 * k
     summed = jnp.ones((SUM_ROWS, tile), jnp.bfloat16)
 
-    def attend(i, d):
+    def attend(i, d, ways):
         on_q = jnp.where((i == 0) | (i == 3) | (i == 4), 2, jnp.where((i == 2) | (i == 6), outer, inner))
         on_kv = jnp.where(
             i <= 2,
@@ -415,8 +415,6 @@
         def side(way):
             layer_step, row_step = steps_to(d, way)
             place = (layer_step + 1) * 9 + (row_step + 1) * 3 + shift + 1
-            if way == 1:
-                place = jnp.where(d == 0, FLAG_ROWS - 1, place)
             there = used(d, way)
             slot = jnp.where(there, slot_of(d, way), 0)
             at = jnp.where(there | (d == 0), on_kv, jnp.minimum(on_kv, 2))
@@ -435,9 +433,11 @@
             )
             return live, scores, top, jnp.concatenate([turned, summed], axis=0)
 
-        sides = [side(0), side(1)]
+        sides = [side(way) for way in ways]
         before = peak[on_q]
-        now = jnp.maximum(before, jnp.maximum(sides[0][2], sides[1][2]))
+        now = before
+        for _, _, top, _ in sides:
+            now = jnp.maximum(now, top)
         result = total[on_q] * jnp.exp2((before - now) * EXPONENT_SCALE)
         for live, scores, _, turned in sides:
             base = jnp.where(live, now, -LOW)
@@ -544,7 +544,13 @@
             def _():
                 await_extra(0)
 
-            attend(i, plane)
+            @pl.when(plane == 0)
+            def _():
+                attend(i, plane, (0,))
+
+            @pl.when(plane > 0)
+            def _():
+                attend(i, plane, (0, 1))
 
             @pl.when((plane == far) & ((i == 4) | (i >= 6)))
             def _():

time: 86.4 us -> 86.4 us (level)
  no operation moved by 1% of the time
where the time goes in v4:
time: 86.4 us; the launch traced here: 86.3 us
  Pallas kernels  84.9 us (98%)
    pallas_call x1, Pallas kernels, attention(): pl.pallas_call(functools.partial(kernel, rows_of_tiles, frames, parts), o...  84.9 us

profile of v4, /device:TPU:129, one launch (start us, length us, event | category | flops | bytes accessed | tf_op | source)
XLA Modules:
  0.0 86.3 jit_solution(5263991136939990255)
XLA Ops:
  0.7 84.9 %shard_map.55 = bf16[48,3072]{1,0:T(8,128)(2,1)S(1)} custom-call(s32[1,27]{1,0:T(1,128)} %windows.1, s32[1,1]{1,0:T(1,128)} %bitcast.1.counts, bf16[48,3072]{1,0:T(8,128)(2,1)} %queries.1, bf16[48,3072]{1,0:T(8,128)(2,1)} %keys.1, bf16[48,3072]{1,0:T(8,128)(2,1)} %values.1), custom_call_target="tpu_custom_call" | custom-call | tf_op jit(solution)/shard_map/pallas_call | solution.py:644
  85.5 0.7 copy.7
